TPU v7x, 32 devices: a whole 2x2x4 slice. The times are simulated.
32 devices in a mesh: patch: 8 (over z, x), tile: 4 (over y, core).
Axes of the slice: x: 2, y: 2, z: 4, core: 2. Of those that a mesh axis runs over, the one named last changes fastest.
Arguments:
- latents: float32 [1088, 128], P('patch')
- timestamps: int32 [1088], P('patch'), may hold values from 0 to 56, as said below
- cell_map: int32 [1024], replicated, may hold values from 0 to 1023, as said below
- w_video: bfloat16 [128, 3072], replicated, may hold values from -0.5 to 0.5
- w_audio: bfloat16 [128, 3072], replicated, may hold values from -0.5 to 0.5
- mod_scale: float32 [2, 3072], replicated, may hold values from -3 to 3
- mod_shift: float32 [2, 3072], replicated, may hold values from -3 to 3
- w_query: bfloat16 [3072, 3072], P(None, 'tile')
- w_key: bfloat16 [3072, 3072], P(None, 'tile')
- w_value: bfloat16 [3072, 3072], P(None, 'tile'), may hold values from -0.109375 to 0.109375
- q_gain: float32 [3072], P('tile'), as said below
- k_gain: float32 [3072], P('tile'), as said below
- k_cache: bfloat16 [1088, 3072], P('patch', 'tile'), may hold values from -8 to 8
- v_cache: bfloat16 [1088, 3072], P('patch', 'tile'), may hold values from -6 to 6
- w_out: bfloat16 [3072, 3072], P('tile'), may hold values from -0.109375 to 0.109375
- out_gain: float32 [3072], replicated, may hold values from 0.25 to 1.75
- w_final: bfloat16 [3072, 128], replicated, may hold values from -0.109375 to 0.109375
- step_sizes: float32 [2], replicated, may hold values from 0.2 to 0.6
- conv_w: bfloat16 [3, 3, 3, 128, 512], replicated, may hold values from -0.109375 to 0.109375
- conv_b: float32 [512], replicated, may hold values from -3 to 3
Outputs:
- final_latents: float32 [1088, 128], P('patch')
- decoded: bfloat16 [8, 16, 8, 512], P(None, 'patch', 'tile')
Inputs may be any that keep to these rules, and one draw needn't show every extreme that they name: `cell_map`: a permutation of the 1024 cells of the grid; entry r is the cell of the r-th video token, which stands in patch shard r // 128; cell (f, h, w) belongs to the decode block (h // 2, w // 2), held by patch index h // 2 and tile index w // 2; every patch shard holds exactly 4 cells of every decode block. A video token's timestamp is 8 times the frame of its cell; audio tokens' timestamps lie in the same span. `q_gain`: positive. `k_gain`: positive.
All inputs are finite; a program needn't handle non-finite values.
Results may differ from a plain program's by a relative error of at most 0.009.
Values may be sent and summed in bfloat16 or wider, within the bound.
A program may use at most 128 MiB of HBM per device.

v0:
```python
import jax
import jax.numpy as jnp
from jax import lax
from jax.sharding import PartitionSpec as P

HEAD = 128
VID_DEV = 128
STEPS = 2
FRAMES = 8
BH = 2
EPSILON = 1e-06


def with_halo(shard, sides, width):
    for axis, dim in sides:
        count, length = (lax.axis_size(axis), shard.shape[dim])
        up = [(i, (i + 1) % count) for i in range(count - 1)]
        down = [(j, i) for i, j in up]
        last = lax.slice_in_dim(shard, length - width, length, axis=dim)
        first = lax.slice_in_dim(shard, 0, width, axis=dim)
        before = lax.ppermute(last, axis, up)
        after = lax.ppermute(first, axis, down)
        shard = jnp.concatenate([before, shard, after], axis=dim)
    return shard


def row_scaled(matrix):
    return matrix * lax.rsqrt(jnp.mean(matrix * matrix, axis=-1, keepdims=True) + EPSILON)


def rotate(matrix, stamps):
    half_size = matrix.shape[-1] // 2
    frequency = jnp.exp(-jnp.log(10000.0) * jnp.arange(half_size, dtype=jnp.float32) / half_size)
    angles = stamps.astype(jnp.float32)[:, None, None] * frequency
    cosine = jnp.cos(angles)
    sines = jnp.sin(angles)
    leading = matrix[..., :half_size]
    trailing = matrix[..., half_size:]
    return jnp.concatenate(
        [leading * cosine - trailing * sines, leading * sines + trailing * cosine], axis=-1
    )


def head_project(normed, weight, gain, stamps):
    raw_out = jnp.dot(normed, weight, preferred_element_type=jnp.float32)
    shaped = raw_out.reshape(raw_out.shape[0], -1, HEAD)
    scaled = row_scaled(shaped) * gain.reshape(-1, HEAD)
    return rotate(scaled, stamps).reshape(raw_out.shape[0], -1).astype(jnp.bfloat16)


def attend_whole(queries, fresh_keys, values, stale_keys, stale_values, row_start):
    every_keys, every_values = (
        lax.all_gather(stale_keys, "patch", axis=0, tiled=True),
        lax.all_gather(stale_values, "patch", axis=0, tiled=True),
    )
    every_keys = lax.dynamic_update_slice_in_dim(every_keys, fresh_keys, row_start, 0)
    every_values = lax.dynamic_update_slice_in_dim(every_values, values, row_start, 0)
    row_count = queries.shape[0]
    query_heads = queries.reshape(row_count, -1, HEAD)
    key_heads = every_keys.reshape(every_keys.shape[0], -1, HEAD)
    value_heads = every_values.reshape(every_values.shape[0], -1, HEAD)
    scores = jnp.einsum(
        "qhd,khd->hqk", query_heads, key_heads, preferred_element_type=jnp.float32
    ) * HEAD ** (-0.5)
    row_top = jnp.max(scores, axis=2, keepdims=True)
    weights = jnp.exp(scores - row_top)
    totals = jnp.sum(weights, axis=2)
    result = jnp.einsum(
        "hqk,khd->qhd",
        weights.astype(jnp.bfloat16),
        value_heads,
        preferred_element_type=jnp.float32,
    )
    return (result / totals.T[:, :, None]).reshape(row_count, -1).astype(jnp.bfloat16)


def velocity_of(embedded, attended, w_out, out_gain, w_final):
    share_rows = attended.shape[0] // lax.axis_size("tile")
    own_rows = lax.dynamic_slice_in_dim(
        embedded, lax.axis_index("tile") * share_rows, share_rows, 0
    )
    mixed_rows = own_rows + lax.psum_scatter(
        jnp.dot(attended, w_out, preferred_element_type=jnp.float32).astype(jnp.bfloat16),
        "tile",
        scatter_dimension=0,
        tiled=True,
    ).astype(jnp.float32)
    final_normed = (row_scaled(mixed_rows) * out_gain).astype(jnp.bfloat16)
    own_velocity = jnp.dot(final_normed, w_final, preferred_element_type=jnp.float32)
    return lax.all_gather(own_velocity, "tile", axis=0, tiled=True)


def decode(latent_state, cell_map, conv_w, conv_b):
    video_rows = latent_state[:VID_DEV].astype(jnp.bfloat16)
    patch_count = lax.axis_size("patch")
    tile_count = lax.axis_size("tile")
    patch_index = lax.axis_index("patch")
    tile_index = lax.axis_index("tile")
    block_width = VID_DEV // (tile_count * FRAMES * BH)
    grid_rows = BH * patch_count
    grid_columns = block_width * tile_count
    cell_count = FRAMES * BH * block_width
    local_cells = jnp.arange(cell_count, dtype=jnp.int32)
    frame_ids = local_cells // (BH * block_width)
    inner_row = local_cells // block_width % BH
    inner_column = local_cells % block_width
    own_cells = (
        (frame_ids * grid_rows + patch_index * BH + inner_row) * grid_columns
        + tile_index * block_width
        + inner_column
    )
    matches = cell_map[None, :] == own_cells[:, None]
    every_video = lax.all_gather(video_rows, "patch", axis=0, tiled=True)
    sources = jnp.sum(
        jnp.where(matches, jnp.arange(cell_map.shape[0], dtype=jnp.int32)[None, :], 0), axis=1
    )
    block = every_video[sources]
    block = block.reshape(FRAMES, BH, block_width, -1)
    grown = with_halo(block, (("patch", 1), ("tile", 2)), 1)
    padded = jnp.pad(grown, ((1, 1), (0, 0), (0, 0), (0, 0)))
    columns = jnp.concatenate(
        [
            padded[
                shift_time : shift_time + FRAMES,
                shift_row : shift_row + BH,
                shift_column : shift_column + block_width,
            ]
            for shift_time in range(3)
            for shift_row in range(3)
            for shift_column in range(3)
        ],
        axis=-1,
    )
    kernel = conv_w.reshape(-1, conv_w.shape[-1])
    conv_out = (
        jnp.dot(columns.reshape(cell_count, -1), kernel, preferred_element_type=jnp.float32)
        + conv_b
    )
    return conv_out.astype(jnp.bfloat16).reshape(FRAMES, BH, block_width, -1)


def local(
    latents,
    timestamps,
    cell_map,
    w_video,
    w_audio,
    mod_scale,
    mod_shift,
    w_query,
    w_key,
    w_value,
    q_gain,
    k_gain,
    k_cache,
    v_cache,
    w_out,
    out_gain,
    w_final,
    step_sizes,
    conv_w,
    conv_b,
):
    row_count = latents.shape[0]
    row_start = lax.axis_index("patch") * row_count
    latent_state = latents
    stale_keys = k_cache
    stale_values = v_cache
    for step_index in range(STEPS):
        latent_b = latent_state.astype(jnp.bfloat16)
        video_part = jnp.dot(latent_b[:VID_DEV], w_video, preferred_element_type=jnp.float32)
        audio_part = jnp.dot(latent_b[VID_DEV:], w_audio, preferred_element_type=jnp.float32)
        embedded = jnp.concatenate([video_part, audio_part], axis=0)
        normed = (
            row_scaled(embedded) * (1.0 + mod_scale[step_index]) + mod_shift[step_index]
        ).astype(jnp.bfloat16)
        queries = head_project(normed, w_query, q_gain, timestamps)
        fresh_keys = head_project(normed, w_key, k_gain, timestamps)
        values = jnp.dot(normed, w_value, preferred_element_type=jnp.float32).astype(jnp.bfloat16)
        attended = attend_whole(queries, fresh_keys, values, stale_keys, stale_values, row_start)
        velocity = velocity_of(embedded, attended, w_out, out_gain, w_final)
        latent_state = latent_state - step_sizes[step_index] * velocity
        stale_keys = fresh_keys
        stale_values = values
    decoded = decode(latent_state, cell_map, conv_w, conv_b)
    return (latent_state, decoded)


def solution(mesh):
    return jax.shard_map(
        local,
        mesh=mesh,
        in_specs=(
            P("patch", None),
            P("patch"),
            P(),
            P(),
            P(),
            P(),
            P(),
            P(None, "tile"),
            P(None, "tile"),
            P(None, "tile"),
            P("tile"),
            P("tile"),
            P("patch", "tile"),
            P("patch", "tile"),
            P("tile", None),
            P(),
            P(),
            P(),
            P(),
            P(),
        ),
        out_specs=(P("patch", None), P(None, "patch", "tile", None)),
        check_vma=False,
    )
```

profile of v0, /device:TPU:12, one launch (start us, length us, event | category | flops | bytes accessed | tf_op | source)
XLA Modules:
  0.0 313.6 jit_solution(8176964901523891090)
XLA Ops:
  18.8 1.9 multiply_reduce_fusion.4
  21.7 4.2 %fusion.94 = f32[136,768]{1,0:T(8,128)} fusion(bf16[136,3072]{1,0:T(8,128)(2,1)} %copy-done.7, bf16[3072,768]{1,0:T(8,128)(2,1)} %param.27), kind=kOutput, calls=%fused_computation.194 | convolution fusion | flops 641728512 | bytes 5971968 | tf_op jit(solution)/shard_map/dot_general | solution.py:45
  38.1 18.7 %all-gather.7.cloned.1.call-done = bf16[1088,768]{1,0:T(8,128)(2,1)} async-done(((bf16[136,768]{1,0:T(8,128)(2,1)}), bf16[1088,768]{1,0:T(8,128)(2,1)}) %all-gather.7.cloned.1.call-update) | async-done | bytes 1671184 | tf_op jit(solution)/shard_map/all_gather | solution.py:54
  56.8 4.2 %constant_dynamic-update-slice_fusion.28 = (bf16[1088,768]{1,0:T(8,128)(2,1)}, bf16[136,768]{1,0:T(8,128)(2,1)}) fusion(bf16[1088,768]{1,0:T(8,128)(2,1)} %all-gather.7.cloned.1.call-done, s32[]{:T(128)S(6)} %select_n.60, bf16[136,3072]{1,0:T(8,128)(2,1)} %copy-done.7, bf16[3072,768]{1,0:T(8,128)(2,1)} %param.29), kind=kOutput, calls=%fused_computation.161 | convolution fusion | flops 641832960 | bytes 5971972 | tf_op jit(solution)/shard_map/dot_general | solution.py:179
  61.0 3.8 %copy.84 = bf16[1088,768]{0,1:T(8,128)(2,1)} copy(bf16[1088,768]{1,0:T(8,128)(2,1)} %get-tuple-element.54) | data formatting | bytes 3342336 | tf_op jit(solution)/shard_map/dynamic_update_slice | solution.py:57
  64.9 38.1 %all-gather.9.cloned.1.call-done = bf16[1088,768]{1,0:T(8,128)(2,1)} async-done(((bf16[136,768]{1,0:T(8,128)(2,1)}), bf16[1088,768]{1,0:T(8,128)(2,1)}) %all-gather.9.cloned.1.call-update) | async-done | bytes 1671184 | tf_op jit(solution)/shard_map/all_gather | solution.py:53
  104.8 3.8 %copy.90 = bf16[1088,768]{0,1:T(8,128)(2,1)} copy(bf16[1088,768]{1,0:T(8,128)(2,1)} %constant_dynamic-update-slice_fusion.27) | data formatting | bytes 3342336 | tf_op jit(solution)/shard_map/dynamic_update_slice | solution.py:56
  108.6 2.7 fusion.92
  115.7 14.3 %fusion = bf16[40,3072]{1,0:T(8,128)(2,1)} fusion(bf16[136,3072]{1,0:T(8,128)(2,1)} %convolution_convert_fusion.1), kind=kCustom, calls=%all-reduce-scatter | all-reduce-scatter fusion | flops 491521 | bytes 1081856
  134.2 4.2 %collective-permute-done.4 = bf16[18,3072]{1,0:T(8,128)(2,1)} collective-permute-done((bf16[18,3072]{1,0:T(8,128)(2,1)}, bf16[18,3072]{1,0:T(8,128)(2,1)}, u32[]{:S(2)}, u32[]{:S(2)}) %collective-permute-start.4) | collective-permute-done | bytes 110624
  138.4 5.4 %concatenate.139 = bf16[58,3072]{1,0:T(8,128)(2,1)} concatenate(bf16[18,3072]{1,0:T(8,128)(2,1)} %collective-permute-done.4, bf16[40,3072]{1,0:T(8,128)(2,1)} %fusion), dimensions={0} | concatenate | bytes 712704
  147.2 5.5 %all-gather = f32[4,34,128]{2,1,0:T(8,128)S(1)} all-gather(f32[1,34,128]{2,1,0:T(8,128)S(1)} %convolution_bitcast_fusion.1), channel_id=1, replica_groups=mesh['patch'=8,'tile'=4] {'tile'}, dimensions={0}, use_global_device_ids=true | all-gather | bytes 87040 | tf_op jit(solution)/shard_map/all_gather | solution.py:90
  162.1 4.0 %fusion.96 = f32[136,768]{1,0:T(8,128)} fusion(bf16[136,3072]{1,0:T(8,128)(2,1)S(1)} %add_convert_fusion, bf16[3072,768]{1,0:T(8,128)(2,1)} %param.27), kind=kOutput, calls=%fused_computation.196 | convolution fusion | flops 641728512 | bytes 5971968 | tf_op jit(solution)/shard_map/dot_general | solution.py:45
  171.4 4.2 %fusion.97 = f32[136,768]{1,0:T(8,128)} fusion(bf16[136,3072]{1,0:T(8,128)(2,1)} %copy-done.8, bf16[3072,768]{1,0:T(8,128)(2,1)} %param.28), kind=kOutput, calls=%fused_computation.197 | convolution fusion | flops 641728512 | bytes 5971968 | tf_op jit(solution)/shard_map/dot_general | solution.py:45
  175.6 1.9 reshape.274
  188.0 3.8 %copy.100 = bf16[1088,768]{0,1:T(8,128)(2,1)} copy(bf16[1088,768]{1,0:T(8,128)(2,1)} %bitcast_dynamic-update-slice_fusion) | data formatting | bytes 3342336 | tf_op jit(solution)/shard_map/dynamic_update_slice | solution.py:56
  191.8 2.6 fusion.93
  197.5 4.1 %fusion.18 = bf16[1088,768]{1,0:T(8,128)(2,1)} fusion(bf16[1088,768]{1,0:T(8,128)(2,1)} %all-gather.11.cloned.1.call-done, s32[]{:T(128)S(6)} %select_n.60, bf16[136,3072]{1,0:T(8,128)(2,1)} %copy-done.8, bf16[3072,768]{1,0:T(8,128)(2,1)} %param.29), kind=kOutput, calls=%fused_computation.28 | convolution fusion | flops 641832960 | bytes 5763076 | tf_op jit(solution)/shard_map/dot_general | solution.py:179
  201.6 3.8 %copy.94 = bf16[1088,768]{0,1:T(8,128)(2,1)} copy(bf16[1088,768]{1,0:T(8,128)(2,1)} %fusion.18) | data formatting | bytes 3342336 | tf_op jit(solution)/shard_map/dynamic_update_slice | solution.py:57
  205.5 3.7 %fusion.34 = bf16[6,17,8,128]{3,2,1,0:T(8,128)(2,1)S(1)} fusion(bf16[1088,6,128]{0,2,1:T(8,128)(2,1)} %bitcast.154, f32[6,136,1088]{2,1,0:T(8,128)} %copy-done.6, f32[6,136]{1,0:T(8,128)} %copy-done.24, f32[136,6]{0,1:T(8,128)} %bitcast.194), kind=kOutput, calls=%fused_computation.35 | convolution fusion | flops 229263360 | bytes 5437824 | tf_op jit(solution)/shard_map/hqk,khd->qhd/dot_general | solution.py:68
  209.2 4.1 %convolution_convert_fusion = bf16[136,3072]{1,0:T(8,128)(2,1)} fusion(bf16[768,3072]{1,0:T(8,128)(2,1)} %param.34, bf16[6,17,8,128]{3,2,1,0:T(8,128)(2,1)S(1)} %fusion.34), kind=kOutput, calls=%fused_computation.5 | convolution fusion | flops 642146304 | bytes 5763072 | tf_op jit(solution)/shard_map/dot_general | solution.py:83
  213.3 15.0 %fusion.1 = bf16[40,3072]{1,0:T(8,128)(2,1)} fusion(bf16[136,3072]{1,0:T(8,128)(2,1)} %convolution_convert_fusion), kind=kCustom, calls=%all-reduce-scatter.1 | all-reduce-scatter fusion | flops 491521 | bytes 1081856
  229.3 1.9 collective-permute-start.5
  231.8 4.0 %collective-permute-done.5 = bf16[18,3072]{1,0:T(8,128)(2,1)} collective-permute-done((bf16[18,3072]{1,0:T(8,128)(2,1)S(1)}, bf16[18,3072]{1,0:T(8,128)(2,1)}, u32[]{:S(2)}, u32[]{:S(2)}) %collective-permute-start.5) | collective-permute-done | bytes 110624
  235.8 5.4 %concatenate.140 = bf16[58,3072]{1,0:T(8,128)(2,1)} concatenate(bf16[18,3072]{1,0:T(8,128)(2,1)} %collective-permute-done.5, bf16[40,3072]{1,0:T(8,128)(2,1)} %fusion.1), dimensions={0} | concatenate | bytes 712704
  244.6 5.3 %all-gather.1 = f32[4,34,128]{2,1,0:T(8,128)S(1)} all-gather(f32[1,34,128]{2,1,0:T(8,128)S(1)} %convolution_bitcast_fusion), channel_id=1, replica_groups=mesh['patch'=8,'tile'=4] {'tile'}, dimensions={0}, use_global_device_ids=true | all-gather | bytes 87040 | tf_op jit(solution)/shard_map/all_gather | solution.py:90
  254.2 29.8 %all_gather.27 = bf16[1024,128]{1,0:T(8,128)(2,1)} all-gather(bf16[128,128]{1,0:T(8,128)(2,1)S(1)} %slice.284), channel_id=1, replica_groups=mesh['patch'=8,'tile'=4] {'patch'}, dimensions={0}, use_global_device_ids=true | all-gather | bytes 294912 | tf_op jit(solution)/shard_map/all_gather | solution.py:113
  285.6 4.6 %collective-permute-start.1 = (bf16[8,1,2,128]{3,2,1,0:T(2,128)(2,1)S(1)}, bf16[8,1,2,128]{3,2,1,0:T(2,128)(2,1)S(1)}, u32[]{:S(2)}, u32[]{:S(2)}) collective-permute-start(bf16[8,1,2,128]{3,2,1,0:T(2,128)(2,1)S(1)} %get-tuple-element.49), channel_id=1, source_target_pairs={{4,0},{8,4},{12,8},{16,12},{20,16},{24,20},{28,24},{5,1},{9,5},{13... | collective-permute-start | bytes 12296 | tf_op jit(solution)/shard_map/ppermute | solution.py:22
  290.3 1.9 collective-permute-start
  292.2 4.5 %collective-permute-done = bf16[8,1,2,128]{3,2,1,0:T(2,128)(2,1)S(1)} collective-permute-done((bf16[8,1,2,128]{3,2,1,0:T(2,128)(2,1)S(1)}, bf16[8,1,2,128]{3,2,1,0:T(2,128)(2,1)S(1)}, u32[]{:S(2)}, u32[]{:S(2)}) %collective-permute-start) | collective-permute-done | bytes 4128 | tf_op jit(solution)/shard_map/ppermute | solution.py:21
  298.7 2.4 collective-permute-start.2
  301.1 2.6 collective-permute-done.2
  (184 shorter events, 82.0 us)
Async XLA Ops:
  7.2 297.2 %copy-start = (bf16[3,3,3,128,512]{4,3,2,1,0:T(8,128)(2,1)S(1)}, bf16[3,3,3,128,512]{4,3,2,1,0:T(8,128)(2,1)}, u32[]{:S(2)}) copy-start(bf16[3,3,3,128,512]{4,3,2,1,0:T(8,128)(2,1)} %param.38) | copy-start | bytes 10616836
  7.2 49.6 %all-gather.7.cloned.1.call-start = ((), (), s32[]{:S(2)}) async-start(), calls=%async_computation | async-start | bytes 1880064 | tf_op jit(solution)/shard_map/all_gather | solution.py:54
  7.9 95.0 %all-gather.9.cloned.1.call-start = ((), (), s32[]{:S(2)}) async-start(), calls=%async_computation.1 | async-start | bytes 1880064 | tf_op jit(solution)/shard_map/all_gather | solution.py:53
  8.7 177.5 %all-gather.13.cloned.1.call-start = ((), (), s32[]{:S(2)}) async-start(), calls=%async_computation.3 | async-start | bytes 1880064 | tf_op jit(solution)/shard_map/all_gather | solution.py:53
  8.7 3.9 %copy-start.25 = (f32[2,3072]{1,0:T(2,128)S(1)}, f32[2,3072]{1,0:T(2,128)}, u32[]{:S(2)}) copy-start(f32[2,3072]{1,0:T(2,128)} %param.26) | copy-start | bytes 73732
  8.7 4.5 %copy-start.26 = (f32[2,3072]{1,0:T(2,128)S(1)}, f32[2,3072]{1,0:T(2,128)}, u32[]{:S(2)}) copy-start(f32[2,3072]{1,0:T(2,128)} %param.25) | copy-start | bytes 73732
  11.0 3.1 copy-start.9
  11.0 4.3 %copy-start.5 = (bf16[3072,768]{1,0:T(8,128)(2,1)S(1)}, bf16[3072,768]{1,0:T(8,128)(2,1)}, u32[]{:S(2)}) copy-start(bf16[3072,768]{1,0:T(8,128)(2,1)} %param.28) | copy-start | bytes 14155780
  31.8 2.7 copy-start.16
  31.8 2.7 copy-start.18
  33.3 2.8 copy-start.28
  33.3 3.6 %copy-start.31 = (u32[32]{0:T(128)S(1)}, u32[32]{0:T(128)}, u32[]{:S(2)}) copy-start(u32[32]{0:T(128)} %constant.105) | copy-start | bytes 388
  36.1 161.4 %all-gather.11.cloned.1.call-start = ((), (), s32[]{:S(2)}) async-start(), calls=%async_computation.2 | async-start | bytes 1880064 | tf_op jit(solution)/shard_map/all_gather | solution.py:54
  108.6 5.4 %slice-start = ((s8[4718592]{0:T(1024)(128)(4,1)}), s8[4194304]{0:T(1024)(128)(4,1)S(1)}, s32[]{:S(2)}) async-start(s8[4718592]{0:T(1024)(128)(4,1)} %bitcast.149), calls=%async_computation.4 | async-start | bytes 8388608
  111.3 2.7 slice-start.1
  114.0 19.5 %copy-start.30 = (f32[2]{0:T(128)S(1)}, f32[2]{0:T(128)}, u32[]{:S(2)}) copy-start(f32[2]{0:T(128)} %param.37) | copy-start | bytes 28
  130.0 15.5 %copy-start.21 = (f32[3072]{0:T(1024)S(1)}, f32[3072]{0:T(1024)}, u32[]{:S(2)}) copy-start(f32[3072]{0:T(1024)} %param.35) | copy-start | bytes 36868
  131.6 6.8 %collective-permute-start.4 = (bf16[18,3072]{1,0:T(8,128)(2,1)}, bf16[18,3072]{1,0:T(8,128)(2,1)}, u32[]{:S(2)}, u32[]{:S(2)}) collective-permute-start(bf16[18,3072]{1,0:T(8,128)(2,1)} %slice.255), channel_id=1, source_target_pairs={{0,1},{1,2},{2,3},{4,5},{5,6},{6,7},{8,9},{9,10},{10,11},{12,13},{... | collective-permute-start | bytes 331784
  158.4 1.8 copy-start.11
  158.4 1.8 copy-start.22
  158.4 1.8 copy-start.23
  171.4 11.1 %copy-start.27 = (f32[768]{0:T(1024)S(1)}, f32[768]{0:T(1024)}, u32[]{:S(2)}) copy-start(f32[768]{0:T(1024)} %param.30) | copy-start | bytes 9220
  181.0 3.8 %copy-start.17 = (f32[136,64]{1,0:T(8,128)S(1)}, f32[136,64]{1,0:T(8,128)}, u32[]{:S(2)}) copy-start(f32[136,64]{1,0:T(8,128)} %copy-done.16) | copy-start | bytes 104452
  181.0 3.8 %copy-start.19 = (f32[136,64]{1,0:T(8,128)S(1)}, f32[136,64]{1,0:T(8,128)}, u32[]{:S(2)}) copy-start(f32[136,64]{1,0:T(8,128)} %copy-done.18) | copy-start | bytes 104452
  194.3 1.8 copy-start.6
  194.3 1.8 copy-start.24
  229.3 6.6 %collective-permute-start.5 = (bf16[18,3072]{1,0:T(8,128)(2,1)S(1)}, bf16[18,3072]{1,0:T(8,128)(2,1)}, u32[]{:S(2)}, u32[]{:S(2)}) collective-permute-start(bf16[18,3072]{1,0:T(8,128)(2,1)S(1)} %slice.256), channel_id=1, source_target_pairs={{0,1},{1,2},{2,3},{4,5},{5,6},{6,7},{8,9},{9,10},{10,11},{12,13},{... | collective-permute-start | bytes 331784
  244.6 59.8 %copy-start.29 = (f32[512]{0:T(512)S(1)}, f32[512]{0:T(512)}, u32[]{:S(2)}) copy-start(f32[512]{0:T(512)} %param.39) | copy-start | bytes 6148
  285.6 6.5 %collective-permute-start.1 = (bf16[8,1,2,128]{3,2,1,0:T(2,128)(2,1)S(1)}, bf16[8,1,2,128]{3,2,1,0:T(2,128)(2,1)S(1)}, u32[]{:S(2)}, u32[]{:S(2)}) collective-permute-start(bf16[8,1,2,128]{3,2,1,0:T(2,128)(2,1)S(1)} %get-tuple-element.49), channel_id=1, source_target_pairs={{4,0},{8,4},{12,8},{16,12},{20,16},{24,20},{28,24},{5,1},{9,5},{13... | collective-permute-start | bytes 12296 | tf_op jit(solution)/shard_map/ppermute | solution.py:22
  290.3 6.4 %collective-permute-start = (bf16[8,1,2,128]{3,2,1,0:T(2,128)(2,1)S(1)}, bf16[8,1,2,128]{3,2,1,0:T(2,128)(2,1)S(1)}, u32[]{:S(2)}, u32[]{:S(2)}) collective-permute-start(bf16[8,1,2,128]{3,2,1,0:T(2,128)(2,1)S(1)} %get-tuple-element.48), channel_id=1, source_target_pairs={{0,4},{4,8},{8,12},{12,16},{16,20},{20,24},{24,28},{1,5},{5,9},{9,... | collective-permute-start | bytes 12296 | tf_op jit(solution)/shard_map/ppermute | solution.py:21
  296.7 4.3 %collective-permute-start.3 = (bf16[8,4,1,128]{3,2,1,0:T(2,128)(2,1)S(1)}, bf16[8,4,1,128]{3,2,1,0:T(2,128)(2,1)S(1)}, u32[]{:S(2)}, u32[]{:S(2)}) collective-permute-start(bf16[8,4,1,128]{3,2,1,0:T(2,128)(2,1)S(1)} %get-tuple-element.45), channel_id=1, source_target_pairs={{1,0},{2,1},{3,2},{5,4},{6,5},{7,6},{9,8},{10,9},{11,10},{13,12},{... | collective-permute-start | bytes 24584 | tf_op jit(solution)/shard_map/ppermute | solution.py:22
  298.7 5.1 %collective-permute-start.2 = (bf16[8,4,1,128]{3,2,1,0:T(2,128)(2,1)S(1)}, bf16[8,4,1,128]{3,2,1,0:T(2,128)(2,1)S(1)}, u32[]{:S(2)}, u32[]{:S(2)}) collective-permute-start(bf16[8,4,1,128]{3,2,1,0:T(2,128)(2,1)S(1)} %get-tuple-element.44), channel_id=1, source_target_pairs={{0,1},{1,2},{2,3},{4,5},{5,6},{6,7},{8,9},{9,10},{10,11},{12,13},{... | collective-permute-start | bytes 24584 | tf_op jit(solution)/shard_map/ppermute | solution.py:21
  (12 other events, 15.3 us)
Sparse Core Ops, SparseCore 0:
  10.2 46.5 all-gather.6
  59.0 43.8 all-gather.8
  105.1 43.8 all-gather.12
  151.1 43.8 all-gather.10
where the time goes:
time: 316 us; the launch traced here: 314 us
  waiting for transfers between devices  73.5 us (23%)
  blocking collectives  69.9 us (22%)
  local copies, waits for them, and re-layouts  56.3 us (18%)
  matrix products  48.8 us (15%)
  other arithmetic  35.3 us (11%)
  between operations  15 us (5%)
  starting transfers between devices  14.8 us (5%)
    all_gather x2, waiting for transfers between devices, attend_whole(): lax.all_gather(stale_keys, 'patch', axis=0, tiled=True)  38.1 us
    all_gather x1, blocking collectives, decode(): every_video = lax.all_gather(video_rows, 'patch', axis=0, tiled=True)  29.8 us
    unnamed x2, blocking collectives  29.3 us
    unnamed x99, local copies, waits for them, and re-layouts  21 us
    all_gather x2, waiting for transfers between devices, attend_whole(): lax.all_gather(stale_values, 'patch', axis=0, tiled=True)  18.7 us
    dot_general x4, matrix products, head_project(): raw_out = jnp.dot(normed, weight, preferred_element_type=jnp.float32)  14 us
    reduce_sum x8, other arithmetic, row_scaled(): jnp.mean(matrix * matrix, axis=-1, keepdims=True) + EPSILON  11.3 us
    all_gather x2, blocking collectives, velocity_of(): return lax.all_gather(own_velocity, 'tile', axis=0, tiled=True)  10.8 us
  transfers between devices with their start and end apart: 10, of which 6 were waited for; matrix products, arithmetic and copies ran while one was open for 36% of the time, Pallas kernels for 0%

commit v1 on v0

--- a/solution.py
+++ b/solution.py
@@ -1,3 +1,4 @@
+import functools
 import jax
 import jax.numpy as jnp
 from jax import lax
@@ -9,6 +10,34 @@
 FRAMES = 8
 BH = 2
 EPSILON = 1e-06
+
+
+def shards_handle(work_x, bus_axis, out_dim):
+    outer = lax.axis_size(bus_axis)
+    v_next = lax.axis_index(bus_axis)
+    latest, clean, found_now = (outer, v_next, work_x.shape[out_dim])
+    inbox = tuple(((ii, (ii + 1) % latest) for ii in range(latest)))
+    vals = tuple(((ii, (ii - 1) % latest) for ii in range(latest)))
+    local_now = jnp.zeros(
+        (*work_x.shape[:out_dim], latest * found_now, *work_x.shape[out_dim + 1 :]), work_x.dtype
+    )
+    local_now = lax.dynamic_update_slice_in_dim(local_now, work_x, clean * found_now, axis=out_dim)
+    tmp = vec_out = work_x
+    now = latest // 2
+    for dev_i in [*range(1, now + 1)]:
+        tmp = lax.ppermute(tmp, perm=inbox, axis_name=bus_axis)
+        local_now = lax.dynamic_update_slice_in_dim(
+            local_now, tmp, (clean - dev_i) % latest * found_now, axis=out_dim
+        )
+        if dev_i < latest - now:
+            vec_out = lax.ppermute(vec_out, bus_axis, perm=vals)
+            local_now = lax.dynamic_update_slice_in_dim(
+                local_now, vec_out, (clean + dev_i) % latest * found_now, axis=out_dim
+            )
+    return local_now
+
+
+ratios_check = functools.partial(shards_handle, bus_axis="patch", out_dim=0)
 
 
 def with_halo(shard, sides, width):
@@ -51,7 +80,7 @@
 def attend_whole(queries, fresh_keys, values, stale_keys, stale_values, row_start):
     every_keys, every_values = (
         lax.all_gather(stale_keys, "patch", axis=0, tiled=True),
-        lax.all_gather(stale_values, "patch", axis=0, tiled=True),
+        ratios_check(stale_values),
     )
     every_keys = lax.dynamic_update_slice_in_dim(every_keys, fresh_keys, row_start, 0)
     every_values = lax.dynamic_update_slice_in_dim(every_values, values, row_start, 0)

time: 316 us -> 407 us (1.29)
  local copies, waits for them, and re-layouts: 56.3 us -> 171 us
  waiting for transfers between devices: 73.5 us -> 29.9 us
  starting transfers between devices: 14.8 us -> 35.9 us
  matrix products: 48.8 us -> 41.3 us
    dynamic_update_slice x0 -> x16, local copies, waits for them, and re-layouts: none -> 80.1 us  [the longest x8 39 us: shards_handle(): lax.dynamic_update_slice_in_dim(local_now, tmp, (clean - dev_i) % latest...]
    all_gather x2, waiting for transfers between devices: 38.1 us -> 0.01 us  [attend_whole(): lax.all_gather(stale_keys, 'patch', axis=0, tiled=True)]
    ppermute x0 -> x14, local copies, waits for them, and re-layouts: none -> 26.1 us  [the longest x8 14.9 us: shards_handle(): tmp = lax.ppermute(tmp, perm=inbox, axis_name=bus_axis)]
    ppermute x0 -> x14, starting transfers between devices: none -> 19.1 us  [the longest x8 12.4 us: shards_handle(): tmp = lax.ppermute(tmp, perm=inbox, axis_name=bus_axis)]
    ppermute x0 -> x14, waiting for transfers between devices: none -> 18.8 us  [the longest x6 12.9 us: shards_handle(): vec_out = lax.ppermute(vec_out, bus_axis, perm=vals)]
    all_gather x2 -> x0, waiting for transfers between devices: 18.7 us -> none  [attend_whole(): lax.all_gather(stale_values, 'patch', axis=0, tiled=True)]
    unnamed x6 -> x4, waiting for transfers between devices: 9.63 us -> 4.01 us
    unnamed x99 -> x104, local copies, waits for them, and re-layouts: 21 us -> 20.8 us
  transfers between devices with their start and end apart: 10 -> 22, of which waited for: 6 -> 6; matrix products, arithmetic and copies ran while one was open for 36% -> 55% of each run, Pallas kernels for 0% -> 0%
where the time goes in v1:
time: 407 us; the launch traced here: 402 us
  local copies, waits for them, and re-layouts  171 us (42%)
  blocking collectives  73.3 us (18%)
  matrix products  41.3 us (10%)
  starting transfers between devices  35.9 us (9%)
  other arithmetic  34.7 us (9%)
  waiting for transfers between devices  29.9 us (7%)
  between operations  15.4 us (4%)
    dynamic_update_slice x8, local copies, waits for them, and re-layouts, shards_handle(): lax.dynamic_update_slice_in_dim(local_now, tmp, (clean - dev_i) % latest...  39 us
    all_gather x1, blocking collectives, decode(): every_video = lax.all_gather(video_rows, 'patch', axis=0, tiled=True)  33.2 us
    dynamic_update_slice x6, local copies, waits for them, and re-layouts, shards_handle(): lax.dynamic_update_slice_in_dim(local_now, vec_out, (clean + dev_i) % lat...  30.8 us
    unnamed x2, blocking collectives  29.2 us
    unnamed x104, local copies, waits for them, and re-layouts  20.8 us
    ppermute x8, local copies, waits for them, and re-layouts, shards_handle(): tmp = lax.ppermute(tmp, perm=inbox, axis_name=bus_axis)  14.9 us
    dot_general x4, matrix products, head_project(): raw_out = jnp.dot(normed, weight, preferred_element_type=jnp.float32)  14.3 us
    ppermute x6, waiting for transfers between devices, shards_handle(): vec_out = lax.ppermute(vec_out, bus_axis, perm=vals)  12.9 us
  transfers between devices with their start and end apart: 22, of which 6 were waited for; matrix products, arithmetic and copies ran while one was open for 55% of the time, Pallas kernels for 0%

profile of v1, /device:TPU:12, one launch (start us, length us, event | category | flops | bytes accessed | tf_op | source)
XLA Modules:
  0.0 401.9 jit_solution(17884331751384168004)
XLA Ops:
  26.9 4.2 %fusion.93 = f32[136,768]{1,0:T(8,128)} fusion(bf16[136,3072]{1,0:T(8,128)(2,1)} %copy-done.7, bf16[3072,768]{1,0:T(8,128)(2,1)} %param.27), kind=kOutput, calls=%fused_computation.192 | convolution fusion | flops 641728512 | bytes 5971968 | tf_op jit(solution)/shard_map/dot_general | solution.py:74
  47.7 5.1 %dynamic_update_slice.60 = bf16[1088,768]{0,1:T(8,128)(2,1)} dynamic-update-slice(bf16[1088,768]{0,1:T(8,128)(2,1)} %broadcast.302.clone, bf16[136,768]{0,1:T(8,128)(2,1)} %copy.130, s32[]{:T(128)S(6)} %select_n.134, s32[]{:T(128)} %constant.135.clone.1) | dynamic-update-slice | bytes 417796 | tf_op jit(solution)/shard_map/dynamic_update_slice | solution.py:24
  54.2 5.2 %dynamic_update_slice.70 = bf16[1088,768]{0,1:T(8,128)(2,1)} dynamic-update-slice(bf16[1088,768]{0,1:T(8,128)(2,1)} %broadcast.302.clone.1, bf16[136,768]{0,1:T(8,128)(2,1)} %copy.138, s32[]{:T(128)S(6)} %select_n.134, s32[]{:T(128)} %constant.135.clone.1) | dynamic-update-slice | bytes 417796 | tf_op jit(solution)/shard_map/dynamic_update_slice | solution.py:24
  65.5 12.9 %collective-permute-done.3 = bf16[136,768]{1,0:T(8,128)(2,1)} collective-permute-done((bf16[136,768]{1,0:T(8,128)(2,1)}, bf16[136,768]{1,0:T(8,128)(2,1)}, u32[]{:S(2)}, u32[]{:S(2)}) %collective-permute-start.3) | collective-permute-done | bytes 208928 | tf_op jit(solution)/shard_map/ppermute | solution.py:33
  82.6 4.2 %collective-permute-done.4 = bf16[136,768]{1,0:T(8,128)(2,1)} collective-permute-done((bf16[136,768]{1,0:T(8,128)(2,1)}, bf16[136,768]{1,0:T(8,128)(2,1)}, u32[]{:S(2)}, u32[]{:S(2)}) %collective-permute-start.4) | collective-permute-done | bytes 208928 | tf_op jit(solution)/shard_map/ppermute | solution.py:28
  91.7 5.1 %dynamic_update_slice.61 = bf16[1088,768]{0,1:T(8,128)(2,1)} dynamic-update-slice(bf16[1088,768]{0,1:T(8,128)(2,1)} %dynamic_update_slice.60, bf16[136,768]{0,1:T(8,128)(2,1)} %copy.131, s32[]{:T(128)S(6)} %select_n.136, s32[]{:T(128)} %constant.135.clone.1) | dynamic-update-slice | bytes 417796 | tf_op jit(solution)/shard_map/dynamic_update_slice | solution.py:29
  98.7 5.1 %dynamic_update_slice.62 = bf16[1088,768]{0,1:T(8,128)(2,1)} dynamic-update-slice(bf16[1088,768]{0,1:T(8,128)(2,1)} %dynamic_update_slice.61, bf16[136,768]{0,1:T(8,128)(2,1)} %copy.132, s32[]{:T(128)S(6)} %select_n.138, s32[]{:T(128)} %constant.135.clone.1) | dynamic-update-slice | bytes 417796 | tf_op jit(solution)/shard_map/dynamic_update_slice | solution.py:34
  105.7 4.7 %dynamic_update_slice.63 = bf16[1088,768]{0,1:T(8,128)(2,1)} dynamic-update-slice(bf16[1088,768]{0,1:T(8,128)(2,1)} %dynamic_update_slice.62, bf16[136,768]{0,1:T(8,128)(2,1)} %copy.133, s32[]{:T(128)S(6)} %select_n.140, s32[]{:T(128)} %constant.135.clone.1) | dynamic-update-slice | bytes 417796 | tf_op jit(solution)/shard_map/dynamic_update_slice | solution.py:29
  112.2 5.1 %dynamic_update_slice.64 = bf16[1088,768]{0,1:T(8,128)(2,1)} dynamic-update-slice(bf16[1088,768]{0,1:T(8,128)(2,1)} %dynamic_update_slice.63, bf16[136,768]{0,1:T(8,128)(2,1)} %copy.134, s32[]{:T(128)S(6)} %select_n.142, s32[]{:T(128)} %constant.135.clone.1) | dynamic-update-slice | bytes 417796 | tf_op jit(solution)/shard_map/dynamic_update_slice | solution.py:34
  119.3 4.6 %dynamic_update_slice.65 = bf16[1088,768]{0,1:T(8,128)(2,1)} dynamic-update-slice(bf16[1088,768]{0,1:T(8,128)(2,1)} %dynamic_update_slice.64, bf16[136,768]{0,1:T(8,128)(2,1)} %copy.135, s32[]{:T(128)S(6)} %select_n.144, s32[]{:T(128)} %constant.135.clone.1) | dynamic-update-slice | bytes 417796 | tf_op jit(solution)/shard_map/dynamic_update_slice | solution.py:29
  125.7 5.1 %dynamic_update_slice.66 = bf16[1088,768]{0,1:T(8,128)(2,1)} dynamic-update-slice(bf16[1088,768]{0,1:T(8,128)(2,1)} %dynamic_update_slice.65, bf16[136,768]{0,1:T(8,128)(2,1)} %copy.136, s32[]{:T(128)S(6)} %select_n.146, s32[]{:T(128)} %constant.135.clone.1) | dynamic-update-slice | bytes 417796 | tf_op jit(solution)/shard_map/dynamic_update_slice | solution.py:34
  134.8 5.1 %dynamic_update_slice.67 = bf16[1088,768]{0,1:T(8,128)(2,1)} dynamic-update-slice(bf16[1088,768]{0,1:T(8,128)(2,1)} %dynamic_update_slice.66, bf16[136,768]{0,1:T(8,128)(2,1)} %copy.137, s32[]{:T(128)S(6)} %select_n.148, s32[]{:T(128)} %constant.135.clone.1) | dynamic-update-slice | bytes 417796 | tf_op jit(solution)/shard_map/dynamic_update_slice | solution.py:29
  139.9 5.1 %dynamic_update_slice.68 = bf16[1088,768]{0,1:T(8,128)(2,1)} dynamic-update-slice(bf16[1088,768]{0,1:T(8,128)(2,1)} %dynamic_update_slice.67, bf16[136,768]{0,1:T(8,128)(2,1)} %copy.138, s32[]{:T(128)S(6)} %select_n.134, s32[]{:T(128)} %constant.135.clone.1) | dynamic-update-slice | bytes 417796 | tf_op jit(solution)/shard_map/dynamic_update_slice | solution.py:86
  157.8 13.9 %fusion = bf16[40,3072]{1,0:T(8,128)(2,1)} fusion(bf16[136,3072]{1,0:T(8,128)(2,1)} %convolution_convert_fusion.1), kind=kCustom, calls=%all-reduce-scatter | all-reduce-scatter fusion | flops 491521 | bytes 1081856
  177.7 5.2 %dynamic_update_slice.71 = bf16[1088,768]{0,1:T(8,128)(2,1)} dynamic-update-slice(bf16[1088,768]{0,1:T(8,128)(2,1)} %dynamic_update_slice.70, bf16[136,768]{0,1:T(8,128)(2,1)} %copy.149, s32[]{:T(128)S(6)} %select_n.136, s32[]{:T(128)} %constant.135.clone.1) | dynamic-update-slice | bytes 417796 | tf_op jit(solution)/shard_map/dynamic_update_slice | solution.py:29
  184.8 5.1 %dynamic_update_slice.72 = bf16[1088,768]{0,1:T(8,128)(2,1)} dynamic-update-slice(bf16[1088,768]{0,1:T(8,128)(2,1)} %dynamic_update_slice.71, bf16[136,768]{0,1:T(8,128)(2,1)} %copy.150, s32[]{:T(128)S(6)} %select_n.138, s32[]{:T(128)} %constant.135.clone.1) | dynamic-update-slice | bytes 417796 | tf_op jit(solution)/shard_map/dynamic_update_slice | solution.py:34
  191.8 4.7 %dynamic_update_slice.73 = bf16[1088,768]{0,1:T(8,128)(2,1)} dynamic-update-slice(bf16[1088,768]{0,1:T(8,128)(2,1)} %dynamic_update_slice.72, bf16[136,768]{0,1:T(8,128)(2,1)} %copy.151, s32[]{:T(128)S(6)} %select_n.140, s32[]{:T(128)} %constant.135.clone.1) | dynamic-update-slice | bytes 417796 | tf_op jit(solution)/shard_map/dynamic_update_slice | solution.py:29
  198.3 5.2 %dynamic_update_slice.74 = bf16[1088,768]{0,1:T(8,128)(2,1)} dynamic-update-slice(bf16[1088,768]{0,1:T(8,128)(2,1)} %dynamic_update_slice.73, bf16[136,768]{0,1:T(8,128)(2,1)} %copy.152, s32[]{:T(128)S(6)} %select_n.142, s32[]{:T(128)} %constant.135.clone.1) | dynamic-update-slice | bytes 417796 | tf_op jit(solution)/shard_map/dynamic_update_slice | solution.py:34
  205.3 4.6 %dynamic_update_slice.75 = bf16[1088,768]{0,1:T(8,128)(2,1)} dynamic-update-slice(bf16[1088,768]{0,1:T(8,128)(2,1)} %dynamic_update_slice.74, bf16[136,768]{0,1:T(8,128)(2,1)} %copy.153, s32[]{:T(128)S(6)} %select_n.144, s32[]{:T(128)} %constant.135.clone.1) | dynamic-update-slice | bytes 417796 | tf_op jit(solution)/shard_map/dynamic_update_slice | solution.py:29
  211.8 5.2 %dynamic_update_slice.76 = bf16[1088,768]{0,1:T(8,128)(2,1)} dynamic-update-slice(bf16[1088,768]{0,1:T(8,128)(2,1)} %dynamic_update_slice.75, bf16[136,768]{0,1:T(8,128)(2,1)} %copy.154, s32[]{:T(128)S(6)} %select_n.146, s32[]{:T(128)} %constant.135.clone.1) | dynamic-update-slice | bytes 417796 | tf_op jit(solution)/shard_map/dynamic_update_slice | solution.py:34
  218.8 5.1 %dynamic_update_slice.77 = bf16[1088,768]{0,1:T(8,128)(2,1)} dynamic-update-slice(bf16[1088,768]{0,1:T(8,128)(2,1)} %dynamic_update_slice.76, bf16[136,768]{0,1:T(8,128)(2,1)} %copy.155, s32[]{:T(128)S(6)} %select_n.148, s32[]{:T(128)} %constant.135.clone.1) | dynamic-update-slice | bytes 417796 | tf_op jit(solution)/shard_map/dynamic_update_slice | solution.py:29
  223.9 5.4 %concatenate.139 = bf16[58,3072]{1,0:T(8,128)(2,1)} concatenate(bf16[18,3072]{1,0:T(8,128)(2,1)} %collective-permute-done.18, bf16[40,3072]{1,0:T(8,128)(2,1)} %fusion), dimensions={0} | concatenate | bytes 712704
  232.7 5.6 %all-gather = f32[4,34,128]{2,1,0:T(8,128)S(1)} all-gather(f32[1,34,128]{2,1,0:T(8,128)S(1)} %convolution_bitcast_fusion.1), channel_id=1, replica_groups=mesh['patch'=8,'tile'=4] {'tile'}, dimensions={0}, use_global_device_ids=true | all-gather | bytes 87040 | tf_op jit(solution)/shard_map/all_gather | solution.py:119
  253.3 4.2 %fusion.95 = f32[136,768]{1,0:T(8,128)} fusion(bf16[136,3072]{1,0:T(8,128)(2,1)} %copy-done.8, bf16[3072,768]{1,0:T(8,128)(2,1)} %param.27), kind=kOutput, calls=%fused_computation.194 | convolution fusion | flops 641728512 | bytes 5971968 | tf_op jit(solution)/shard_map/dot_general | solution.py:74
  262.9 4.2 %fusion.96 = f32[136,768]{1,0:T(8,128)} fusion(bf16[136,3072]{1,0:T(8,128)(2,1)} %copy-done.8, bf16[3072,768]{1,0:T(8,128)(2,1)} %param.28), kind=kOutput, calls=%fused_computation.195 | convolution fusion | flops 641728512 | bytes 5971968 | tf_op jit(solution)/shard_map/dot_general | solution.py:74
  283.3 5.1 %dynamic_update_slice.78 = bf16[1088,768]{0,1:T(8,128)(2,1)} dynamic-update-slice(bf16[1088,768]{0,1:T(8,128)(2,1)} %dynamic_update_slice.77, bf16[136,768]{0,1:T(8,128)(2,1)} %copy.156, s32[]{:T(128)S(6)} %select_n.134, s32[]{:T(128)} %constant.135.clone.1) | dynamic-update-slice | bytes 417796 | tf_op jit(solution)/shard_map/dynamic_update_slice | solution.py:86
  295.6 15.3 %fusion.1 = bf16[40,3072]{1,0:T(8,128)(2,1)} fusion(bf16[136,3072]{1,0:T(8,128)(2,1)} %convolution_convert_fusion), kind=kCustom, calls=%all-reduce-scatter.1 | all-reduce-scatter fusion | flops 491521 | bytes 1081856
  318.4 5.4 %concatenate.140 = bf16[58,3072]{1,0:T(8,128)(2,1)} concatenate(bf16[18,3072]{1,0:T(8,128)(2,1)} %collective-permute-done.19, bf16[40,3072]{1,0:T(8,128)(2,1)} %fusion.1), dimensions={0} | concatenate | bytes 712704
  327.2 5.3 %all-gather.1 = f32[4,34,128]{2,1,0:T(8,128)S(1)} all-gather(f32[1,34,128]{2,1,0:T(8,128)S(1)} %convolution_bitcast_fusion), channel_id=1, replica_groups=mesh['patch'=8,'tile'=4] {'tile'}, dimensions={0}, use_global_device_ids=true | all-gather | bytes 87040 | tf_op jit(solution)/shard_map/all_gather | solution.py:119
  336.8 33.2 %all_gather.19 = bf16[1024,128]{1,0:T(8,128)(2,1)} all-gather(bf16[128,128]{1,0:T(8,128)(2,1)S(1)} %slice.284), channel_id=1, replica_groups=mesh['patch'=8,'tile'=4] {'patch'}, dimensions={0}, use_global_device_ids=true | all-gather | bytes 294912 | tf_op jit(solution)/shard_map/all_gather | solution.py:142
  371.6 6.6 %collective-permute-start.15 = (bf16[8,1,2,128]{3,2,1,0:T(2,128)(2,1)S(1)}, bf16[8,1,2,128]{3,2,1,0:T(2,128)(2,1)S(1)}, u32[]{:S(2)}, u32[]{:S(2)}) collective-permute-start(bf16[8,1,2,128]{3,2,1,0:T(2,128)(2,1)S(1)} %get-tuple-element.49), channel_id=1, source_target_pairs={{4,0},{8,4},{12,8},{16,12},{20,16},{24,20},{28,24},{5,1},{9,5},{13... | collective-permute-start | bytes 12296 | tf_op jit(solution)/shard_map/ppermute | solution.py:51
  380.1 4.5 %collective-permute-done.14 = bf16[8,1,2,128]{3,2,1,0:T(2,128)(2,1)S(1)} collective-permute-done((bf16[8,1,2,128]{3,2,1,0:T(2,128)(2,1)S(1)}, bf16[8,1,2,128]{3,2,1,0:T(2,128)(2,1)S(1)}, u32[]{:S(2)}, u32[]{:S(2)}) %collective-permute-start.14) | collective-permute-done | bytes 4128 | tf_op jit(solution)/shard_map/ppermute | solution.py:50
  (246 shorter events, 171.2 us)
Async XLA Ops:
  7.2 385.1 %copy-start = (bf16[3,3,3,128,512]{4,3,2,1,0:T(8,128)(2,1)S(1)}, bf16[3,3,3,128,512]{4,3,2,1,0:T(8,128)(2,1)}, u32[]{:S(2)}) copy-start(bf16[3,3,3,128,512]{4,3,2,1,0:T(8,128)(2,1)} %param.38) | copy-start | bytes 10616836
  7.2 137.8 %all-gather.5.cloned.1.call-start = ((), (), s32[]{:S(2)}) async-start(), calls=%async_computation | async-start | bytes 1880064 | tf_op jit(solution)/shard_map/all_gather | solution.py:82
  7.2 31.2 %collective-permute-start = (bf16[136,768]{1,0:T(8,128)(2,1)}, bf16[136,768]{1,0:T(8,128)(2,1)}, u32[]{:S(2)}, u32[]{:S(2)}) collective-permute-start(bf16[136,768]{1,0:T(8,128)(2,1)} %param.33), channel_id=1, source_target_pairs={{0,4},{4,8},{8,12},{12,16},{16,20},{20,24},{24,28},{28,0},{1,5},{5... | collective-permute-start | bytes 626696 | tf_op jit(solution)/shard_map/ppermute | solution.py:28
  8.8 50.6 %collective-permute-start.1 = (bf16[136,768]{1,0:T(8,128)(2,1)}, bf16[136,768]{1,0:T(8,128)(2,1)}, u32[]{:S(2)}, u32[]{:S(2)}) collective-permute-start(bf16[136,768]{1,0:T(8,128)(2,1)} %param.33), channel_id=1, source_target_pairs={{0,28},{4,0},{8,4},{12,8},{16,12},{20,16},{24,20},{28,24},{1,29},{... | collective-permute-start | bytes 626696 | tf_op jit(solution)/shard_map/ppermute | solution.py:33
  10.2 267.4 %all-gather.7.cloned.1.call-start = ((), (), s32[]{:S(2)}) async-start(), calls=%async_computation.1 | async-start | bytes 1880064 | tf_op jit(solution)/shard_map/all_gather | solution.py:82
  10.3 4.5 %copy-start.26 = (f32[2,3072]{1,0:T(2,128)S(1)}, f32[2,3072]{1,0:T(2,128)}, u32[]{:S(2)}) copy-start(f32[2,3072]{1,0:T(2,128)} %param.25) | copy-start | bytes 73732
  17.5 44.7 %collective-permute-start.7 = (bf16[136,768]{1,0:T(8,128)(2,1)}, bf16[136,768]{1,0:T(8,128)(2,1)}, u32[]{:S(2)}, u32[]{:S(2)}) collective-permute-start(bf16[136,768]{1,0:T(8,128)(2,1)} %convolution_convert_fusion.3), channel_id=1, source_target_pairs={{0,4},{4,8},{8,12},{12,16},{16,20},{20,24},{24,28},{28,0},{1,5},{5... | collective-permute-start | bytes 626696 | tf_op jit(solution)/shard_map/ppermute | solution.py:28
  18.1 47.3 %collective-permute-start.8 = (bf16[136,768]{1,0:T(8,128)(2,1)}, bf16[136,768]{1,0:T(8,128)(2,1)}, u32[]{:S(2)}, u32[]{:S(2)}) collective-permute-start(bf16[136,768]{1,0:T(8,128)(2,1)} %convolution_convert_fusion.3), channel_id=1, source_target_pairs={{0,28},{4,0},{8,4},{12,8},{16,12},{20,16},{24,20},{28,24},{1,29},{... | collective-permute-start | bytes 626696 | tf_op jit(solution)/shard_map/ppermute | solution.py:33
  38.4 23.9 %collective-permute-start.2 = (bf16[136,768]{1,0:T(8,128)(2,1)}, bf16[136,768]{1,0:T(8,128)(2,1)}, u32[]{:S(2)}, u32[]{:S(2)}) collective-permute-start(bf16[136,768]{1,0:T(8,128)(2,1)} %collective-permute-done), channel_id=1, source_target_pairs={{0,4},{4,8},{8,12},{12,16},{16,20},{20,24},{24,28},{28,0},{1,5},{5... | collective-permute-start | bytes 626696 | tf_op jit(solution)/shard_map/ppermute | solution.py:28
  39.8 5.4 %copy-start.31 = (u32[32]{0:T(128)S(1)}, u32[32]{0:T(128)}, u32[]{:S(2)}) copy-start(u32[32]{0:T(128)} %constant.164) | copy-start | bytes 388
  47.7 17.5 %copy-start.28 = (s32[1024]{0:T(1024)S(1)}, s32[1024]{0:T(1024)}, u32[]{:S(2)}) copy-start(s32[1024]{0:T(1024)} %param.22) | copy-start | bytes 12292
  59.4 19.0 %collective-permute-start.3 = (bf16[136,768]{1,0:T(8,128)(2,1)}, bf16[136,768]{1,0:T(8,128)(2,1)}, u32[]{:S(2)}, u32[]{:S(2)}) collective-permute-start(bf16[136,768]{1,0:T(8,128)(2,1)} %collective-permute-done.1), channel_id=1, source_target_pairs={{0,28},{4,0},{8,4},{12,8},{16,12},{20,16},{24,20},{28,24},{1,29},{... | collective-permute-start | bytes 626696 | tf_op jit(solution)/shard_map/ppermute | solution.py:33
  62.2 17.9 %collective-permute-start.9 = (bf16[136,768]{1,0:T(8,128)(2,1)}, bf16[136,768]{1,0:T(8,128)(2,1)}, u32[]{:S(2)}, u32[]{:S(2)}) collective-permute-start(bf16[136,768]{1,0:T(8,128)(2,1)} %collective-permute-done.7), channel_id=1, source_target_pairs={{0,4},{4,8},{8,12},{12,16},{16,20},{20,24},{24,28},{28,0},{1,5},{5... | collective-permute-start | bytes 626696 | tf_op jit(solution)/shard_map/ppermute | solution.py:28
  62.3 24.5 %collective-permute-start.4 = (bf16[136,768]{1,0:T(8,128)(2,1)}, bf16[136,768]{1,0:T(8,128)(2,1)}, u32[]{:S(2)}, u32[]{:S(2)}) collective-permute-start(bf16[136,768]{1,0:T(8,128)(2,1)} %collective-permute-done.2), channel_id=1, source_target_pairs={{0,4},{4,8},{8,12},{12,16},{16,20},{20,24},{24,28},{28,0},{1,5},{5... | collective-permute-start | bytes 626696 | tf_op jit(solution)/shard_map/ppermute | solution.py:28
  65.4 52.0 %collective-permute-start.10 = (bf16[136,768]{1,0:T(8,128)(2,1)}, bf16[136,768]{1,0:T(8,128)(2,1)}, u32[]{:S(2)}, u32[]{:S(2)}) collective-permute-start(bf16[136,768]{1,0:T(8,128)(2,1)} %collective-permute-done.8), channel_id=1, source_target_pairs={{0,28},{4,0},{8,4},{12,8},{16,12},{20,16},{24,20},{28,24},{1,29},{... | collective-permute-start | bytes 626696 | tf_op jit(solution)/shard_map/ppermute | solution.py:33
  78.4 45.4 %collective-permute-start.5 = (bf16[136,768]{1,0:T(8,128)(2,1)}, bf16[136,768]{1,0:T(8,128)(2,1)}, u32[]{:S(2)}, u32[]{:S(2)}) collective-permute-start(bf16[136,768]{1,0:T(8,128)(2,1)} %collective-permute-done.3), channel_id=1, source_target_pairs={{0,28},{4,0},{8,4},{12,8},{16,12},{20,16},{24,20},{28,24},{1,29},{... | collective-permute-start | bytes 626696 | tf_op jit(solution)/shard_map/ppermute | solution.py:33
  80.1 50.7 %collective-permute-start.11 = (bf16[136,768]{1,0:T(8,128)(2,1)}, bf16[136,768]{1,0:T(8,128)(2,1)}, u32[]{:S(2)}, u32[]{:S(2)}) collective-permute-start(bf16[136,768]{1,0:T(8,128)(2,1)} %collective-permute-done.9), channel_id=1, source_target_pairs={{0,4},{4,8},{8,12},{12,16},{16,20},{20,24},{24,28},{28,0},{1,5},{5... | collective-permute-start | bytes 626696 | tf_op jit(solution)/shard_map/ppermute | solution.py:28
  86.8 46.1 %collective-permute-start.6 = (bf16[136,768]{1,0:T(8,128)(2,1)}, bf16[136,768]{1,0:T(8,128)(2,1)}, u32[]{:S(2)}, u32[]{:S(2)}) collective-permute-start(bf16[136,768]{1,0:T(8,128)(2,1)} %collective-permute-done.4), channel_id=1, source_target_pairs={{0,4},{4,8},{8,12},{12,16},{16,20},{20,24},{24,28},{28,0},{1,5},{5... | collective-permute-start | bytes 626696 | tf_op jit(solution)/shard_map/ppermute | solution.py:28
  117.4 92.5 %collective-permute-start.12 = (bf16[136,768]{1,0:T(8,128)(2,1)}, bf16[136,768]{1,0:T(8,128)(2,1)}, u32[]{:S(2)}, u32[]{:S(2)}) collective-permute-start(bf16[136,768]{1,0:T(8,128)(2,1)} %collective-permute-done.10), channel_id=1, source_target_pairs={{0,28},{4,0},{8,4},{12,8},{16,12},{20,16},{24,20},{28,24},{1,29},{... | collective-permute-start | bytes 626696 | tf_op jit(solution)/shard_map/ppermute | solution.py:33
  130.8 86.1 %collective-permute-start.13 = (bf16[136,768]{1,0:T(8,128)(2,1)}, bf16[136,768]{1,0:T(8,128)(2,1)}, u32[]{:S(2)}, u32[]{:S(2)}) collective-permute-start(bf16[136,768]{1,0:T(8,128)(2,1)} %collective-permute-done.11), channel_id=1, source_target_pairs={{0,4},{4,8},{8,12},{12,16},{16,20},{20,24},{24,28},{28,0},{1,5},{5... | collective-permute-start | bytes 626696 | tf_op jit(solution)/shard_map/ppermute | solution.py:28
  150.7 5.3 %slice-start = ((s8[4718592]{0:T(1024)(128)(4,1)}), s8[4194304]{0:T(1024)(128)(4,1)S(1)}, s32[]{:S(2)}) async-start(s8[4718592]{0:T(1024)(128)(4,1)} %bitcast.149), calls=%async_computation.2 | async-start | bytes 8388608
  156.0 19.2 %copy-start.30 = (f32[2]{0:T(128)S(1)}, f32[2]{0:T(128)}, u32[]{:S(2)}) copy-start(f32[2]{0:T(128)} %param.37) | copy-start | bytes 28
  173.3 50.6 %collective-permute-start.18 = (bf16[18,3072]{1,0:T(8,128)(2,1)}, bf16[18,3072]{1,0:T(8,128)(2,1)}, u32[]{:S(2)}, u32[]{:S(2)}) collective-permute-start(bf16[18,3072]{1,0:T(8,128)(2,1)} %slice.255), channel_id=1, source_target_pairs={{0,1},{1,2},{2,3},{4,5},{5,6},{6,7},{8,9},{9,10},{10,11},{12,13},{... | collective-permute-start | bytes 331784
  218.8 12.2 %copy-start.22 = (f32[3072]{0:T(1024)S(1)}, f32[3072]{0:T(1024)}, u32[]{:S(2)}) copy-start(f32[3072]{0:T(1024)} %param.35) | copy-start | bytes 36868
  262.9 11.0 %copy-start.27 = (f32[768]{0:T(1024)S(1)}, f32[768]{0:T(1024)}, u32[]{:S(2)}) copy-start(f32[768]{0:T(1024)} %param.30) | copy-start | bytes 9220
  288.4 5.3 %slice-start.2 = ((s8[4718592]{0:T(1024)(128)(4,1)}), s8[4194304]{0:T(1024)(128)(4,1)S(1)}, s32[]{:S(2)}) async-start(s8[4718592]{0:T(1024)(128)(4,1)} %bitcast.151), calls=%async_computation.4 | async-start | bytes 8388608
  311.8 6.6 %collective-permute-start.19 = (bf16[18,3072]{1,0:T(8,128)(2,1)S(1)}, bf16[18,3072]{1,0:T(8,128)(2,1)}, u32[]{:S(2)}, u32[]{:S(2)}) collective-permute-start(bf16[18,3072]{1,0:T(8,128)(2,1)S(1)} %slice.256), channel_id=1, source_target_pairs={{0,1},{1,2},{2,3},{4,5},{5,6},{6,7},{8,9},{9,10},{10,11},{12,13},{... | collective-permute-start | bytes 331784
  327.2 65.1 %copy-start.29 = (f32[512]{0:T(512)S(1)}, f32[512]{0:T(512)}, u32[]{:S(2)}) copy-start(f32[512]{0:T(512)} %param.39) | copy-start | bytes 6148
  371.6 8.5 %collective-permute-start.15 = (bf16[8,1,2,128]{3,2,1,0:T(2,128)(2,1)S(1)}, bf16[8,1,2,128]{3,2,1,0:T(2,128)(2,1)S(1)}, u32[]{:S(2)}, u32[]{:S(2)}) collective-permute-start(bf16[8,1,2,128]{3,2,1,0:T(2,128)(2,1)S(1)} %get-tuple-element.49), channel_id=1, source_target_pairs={{4,0},{8,4},{12,8},{16,12},{20,16},{24,20},{28,24},{5,1},{9,5},{13... | collective-permute-start | bytes 12296 | tf_op jit(solution)/shard_map/ppermute | solution.py:51
  378.2 6.4 %collective-permute-start.14 = (bf16[8,1,2,128]{3,2,1,0:T(2,128)(2,1)S(1)}, bf16[8,1,2,128]{3,2,1,0:T(2,128)(2,1)S(1)}, u32[]{:S(2)}, u32[]{:S(2)}) collective-permute-start(bf16[8,1,2,128]{3,2,1,0:T(2,128)(2,1)S(1)} %get-tuple-element.48), channel_id=1, source_target_pairs={{0,4},{4,8},{8,12},{12,16},{16,20},{20,24},{24,28},{1,5},{5,9},{9,... | collective-permute-start | bytes 12296 | tf_op jit(solution)/shard_map/ppermute | solution.py:50
  384.7 4.3 %collective-permute-start.17 = (bf16[8,4,1,128]{3,2,1,0:T(2,128)(2,1)S(1)}, bf16[8,4,1,128]{3,2,1,0:T(2,128)(2,1)S(1)}, u32[]{:S(2)}, u32[]{:S(2)}) collective-permute-start(bf16[8,4,1,128]{3,2,1,0:T(2,128)(2,1)S(1)} %get-tuple-element.45), channel_id=1, source_target_pairs={{1,0},{2,1},{3,2},{5,4},{6,5},{7,6},{9,8},{10,9},{11,10},{13,12},{... | collective-permute-start | bytes 24584 | tf_op jit(solution)/shard_map/ppermute | solution.py:51
  386.6 5.1 %collective-permute-start.16 = (bf16[8,4,1,128]{3,2,1,0:T(2,128)(2,1)S(1)}, bf16[8,4,1,128]{3,2,1,0:T(2,128)(2,1)S(1)}, u32[]{:S(2)}, u32[]{:S(2)}) collective-permute-start(bf16[8,4,1,128]{3,2,1,0:T(2,128)(2,1)S(1)} %get-tuple-element.44), channel_id=1, source_target_pairs={{0,1},{1,2},{2,3},{4,5},{5,6},{6,7},{8,9},{9,10},{10,11},{12,13},{... | collective-permute-start | bytes 24584 | tf_op jit(solution)/shard_map/ppermute | solution.py:50
  (26 other events, 56.3 us)
Sparse Core Ops, SparseCore 0:
  10.3 54.1 all-gather.4
  66.7 49.1 all-gather.6
